TPU v7x, 32 devices: a whole 2x2x4 slice. The times are simulated.
32 devices in a mesh: groups: 2 (over x), head: 16 (over z, y, core).
Axes of the slice: x: 2, y: 2, z: 4, core: 2. Of those that a mesh axis runs over, the one named last changes fastest.
Arguments:
- inputs: bfloat16 [6, 16, 8192], P('groups', None, 'head'), parts along dimension 0, may hold values from -6 to 6
- w_query: bfloat16 [8192, 8192], P(None, 'head'), may hold values from -0.0625 to 0.0625
- w_keyval: bfloat16 [8192, 2048], P(None, 'head'), may hold values from -0.21875 to 0.21875
- w_out: bfloat16 [8192, 8192], P('head'), may hold values from -0.0625 to 0.0625
- prefix_keys: bfloat16 [24576, 1024], P(('groups', 'head')), parts along dimension 0, may hold values from -136 to 136
- prefix_values: bfloat16 [24576, 1024], P(('groups', 'head')), parts along dimension 0, may hold values from -24 to 24
- suffix_keys: bfloat16 [256, 64, 128], P(('groups', 'head')), parts along dimension 0, may hold values from -20 to 20
- suffix_values: bfloat16 [256, 64, 128], P(('groups', 'head')), parts along dimension 0, may hold values from -24 to 24
- page_table: int32 [32, 4], P('groups'), parts along dimension 0, may hold values from 0 to 3, each once within a row
- suffix_len: int32 [32], P('groups'), parts along dimension 0, may hold values from 1 to 64, 640 in all
- parents: int32 [6, 16], P('groups'), parts along dimension 0, may hold values from 0 to 15
Outputs:
- outputs: bfloat16 [6, 16, 8192], P('groups', None, 'head'), parts along dimension 0
There are 2 independent parts, one for each index of `groups`. A program takes and returns all parts, laid end to end along the dimension named above; an argument that names none is the same for every part. Nothing has to cross between parts.
Inputs may be any that keep to these rules, and one draw needn't show every extreme that they name: `page_table`: each row is a permutation of the 4 pages of that beam. `suffix_len`: the largest length is 64.
All inputs are finite; a program needn't handle non-finite values.
Results may differ from a plain program's by a relative error of at most 0.006.
The roundings to bfloat16 on the way count: a program that leaves them out, or rounds other values in their place, can miss the bound.
Values may be sent and summed in bfloat16 or wider, within the bound.
A program may use at most 128 MiB of HBM per device.

v0:
```python
import math

import jax
import jax.numpy as jnp
from jax import lax
from jax.sharding import PartitionSpec as P


def lookup(lookup_table, indices):
    row_count = lookup_table.shape[0]
    matches = indices[:, None] == jnp.arange(row_count, dtype=jnp.int32)[None, :]
    return jnp.sum(jnp.where(matches, lookup_table[None, :], 0), axis=1)


def select_rows(indices, row_count):
    return (indices[:, None] == jnp.arange(row_count, dtype=jnp.int32)[None, :]).astype(
        jnp.bfloat16
    )


def slot_valid(page_table, suffix_len, page_size):
    beam_count, page_count = page_table.shape
    page_ids = jnp.arange(page_count, dtype=jnp.int32)
    matches = page_table[:, :, None] == page_ids[None, None, :]
    logical = jnp.sum(jnp.where(matches, page_ids[None, :, None], 0), axis=1)
    position = (
        logical[:, :, None] * page_size + jnp.arange(page_size, dtype=jnp.int32)[None, None, :]
    )
    return position.reshape(beam_count, page_count * page_size) < suffix_len[:, None]


def place_max(target, block_in, row_start, column_start):
    current = lax.dynamic_slice(target, (row_start, column_start), block_in.shape)
    return lax.dynamic_update_slice(
        target, jnp.maximum(current, block_in), (row_start, column_start)
    )


def place_add(target, block_in, starts):
    current = lax.dynamic_slice(target, starts, block_in.shape)
    return lax.dynamic_update_slice(target, current + block_in, starts)


def local(
    inputs,
    w_query,
    w_keyval,
    w_out,
    prefix_keys,
    prefix_values,
    suffix_keys,
    suffix_values,
    page_table,
    suffix_len,
    parents,
):
    devices = lax.axis_size("head")
    position = lax.axis_index("head")
    steps_total, beam_count, width_local = inputs.shape
    head_dim = suffix_keys.shape[2]
    kv_heads = prefix_keys.shape[1] // head_dim
    own_heads = w_out.shape[0] // head_dim
    all_heads = own_heads * devices
    group_size = all_heads // kv_heads
    own_rows = suffix_keys.shape[0]
    slot_count = suffix_keys.shape[1]
    page_size = slot_count // page_table.shape[1]
    pre_len = prefix_keys.shape[0]
    score_scale = 1.0 / math.sqrt(head_dim)
    my_beam = position * own_rows // kv_heads
    first_kv = position * own_rows % kv_heads
    head_start = position * own_heads
    row_kv = first_kv + jnp.arange(own_rows, dtype=jnp.int32)
    valid_orig = slot_valid(page_table, suffix_len, page_size)
    pre_keys = prefix_keys.reshape(pre_len, kv_heads, head_dim)
    pre_values = prefix_values.reshape(pre_len, kv_heads, head_dim)
    cache_keys = suffix_keys
    cache_values = suffix_values
    valid_now = valid_orig.astype(jnp.bfloat16)
    own_kv = (head_start + jnp.arange(own_heads, dtype=jnp.int32)) // group_size
    own_select = select_rows(own_kv, kv_heads)
    keyval_list = []
    results = []
    for step_index in range(steps_total):
        tokens = inputs[step_index]
        block_in = lax.all_gather(tokens, "head", axis=1, tiled=True)
        query_rows = w_query
        query_local = jnp.dot(block_in, query_rows, preferred_element_type=jnp.float32)
        keyval_local = jnp.dot(block_in, w_keyval, preferred_element_type=jnp.float32)
        query_local = query_local.astype(jnp.bfloat16)
        keyval_local = keyval_local.astype(jnp.bfloat16)
        queries, keyvals = (
            lax.all_gather(query_local, "head", axis=1, tiled=True),
            lax.all_gather(keyval_local, "head", axis=1, tiled=True),
        )
        keyval_list.append(keyvals)
        lineage = [None] * (step_index + 1)
        current = jnp.arange(beam_count, dtype=jnp.int32)
        lineage[step_index] = current
        for later_step in range(step_index, 0, -1):
            current = lookup(parents[later_step], current)
            lineage[later_step - 1] = current
        fresh_rows = jnp.stack(
            [
                jnp.dot(
                    select_rows(lineage[earlier], beam_count),
                    keyval_list[earlier],
                    preferred_element_type=jnp.float32,
                )
                for earlier in range(step_index + 1)
            ]
        ).astype(jnp.bfloat16)
        fresh_count = step_index + 1
        fresh_keys = fresh_rows[:, :, : kv_heads * head_dim].reshape(
            fresh_count, beam_count, kv_heads, head_dim
        )
        fresh_values = fresh_rows[:, :, kv_heads * head_dim :].reshape(
            fresh_count, beam_count, kv_heads, head_dim
        )
        own_fresh_keys = jnp.einsum(
            "nbkd,hk->nbhd", fresh_keys, own_select, preferred_element_type=jnp.float32
        ).astype(jnp.bfloat16)
        own_fresh_values = jnp.einsum(
            "nbkd,hk->nbhd", fresh_values, own_select, preferred_element_type=jnp.float32
        ).astype(jnp.bfloat16)
        query_heads = queries.reshape(beam_count, kv_heads, group_size, head_dim)
        score_pre = (
            jnp.einsum("bkgd,pkd->bkgp", query_heads, pre_keys, preferred_element_type=jnp.float32)
            * score_scale
        )
        local_max = jnp.max(score_pre, axis=3).reshape(beam_count, all_heads)
        query_own = query_local.reshape(beam_count, own_heads, head_dim)
        score_new = (
            jnp.einsum(
                "bhd,nbhd->bhn", query_own, own_fresh_keys, preferred_element_type=jnp.float32
            )
            * score_scale
        )
        local_max = place_max(local_max, jnp.max(score_new, axis=2), 0, head_start)
        source_row = (
            lookup(parents[step_index], jnp.full((own_rows,), my_beam, jnp.int32)) * kv_heads
            + row_kv
        )
        blocks = (
            lax.all_gather(cache_keys, "head", axis=0, tiled=True),
            lax.all_gather(cache_values, "head", axis=0, tiled=True),
        )
        gather_row_count = blocks[0].shape[0]
        matches = (
            source_row[:, None] == jnp.arange(gather_row_count, dtype=jnp.int32)[None, :]
        ).astype(jnp.bfloat16)
        cache_keys = jnp.einsum(
            "rn,nsd->rsd", matches, blocks[0], preferred_element_type=jnp.float32
        ).astype(jnp.bfloat16)
        cache_values = jnp.einsum(
            "rn,nsd->rsd", matches, blocks[1], preferred_element_type=jnp.float32
        ).astype(jnp.bfloat16)
        valid_now = jnp.dot(
            select_rows(parents[step_index], beam_count),
            valid_now,
            preferred_element_type=jnp.float32,
        ).astype(jnp.bfloat16)
        my_slots = lax.dynamic_slice_in_dim(valid_now, my_beam, 1, 0)[0] > 0.5
        query_rows = lax.dynamic_slice(
            query_heads, (my_beam, first_kv, 0, 0), (1, own_rows, group_size, head_dim)
        )[0]
        score_suf = (
            jnp.einsum("rgd,rsd->rgs", query_rows, cache_keys, preferred_element_type=jnp.float32)
            * score_scale
        )
        score_suf = jnp.where(my_slots[None, None, :], score_suf, -jnp.inf)
        local_max = place_max(
            local_max,
            jnp.max(score_suf, axis=2).reshape(1, own_rows * group_size),
            my_beam,
            first_kv * group_size,
        )
        global_max = lax.pmax(local_max, "head")
        reshaped_max = global_max.reshape(beam_count, kv_heads, group_size)
        weight_pre = jnp.exp(score_pre - reshaped_max[..., None])
        weigh_numerator = jnp.einsum(
            "bkgp,pkd->bkgd",
            weight_pre.astype(jnp.bfloat16),
            pre_values,
            preferred_element_type=jnp.float32,
        )
        weigh_numerator = weigh_numerator.reshape(beam_count, all_heads, head_dim)
        denominator = jnp.sum(weight_pre, axis=3).reshape(beam_count, all_heads)
        own_max = lax.dynamic_slice(global_max, (0, head_start), (beam_count, own_heads))
        weight_new = jnp.exp(score_new - own_max[..., None])
        numerator_new = jnp.einsum(
            "bhn,nbhd->bhd",
            weight_new.astype(jnp.bfloat16),
            own_fresh_values,
            preferred_element_type=jnp.float32,
        )
        weigh_numerator = place_add(weigh_numerator, numerator_new, (0, head_start, 0))
        denominator = place_add(denominator, jnp.sum(weight_new, axis=2), (0, head_start))
        suffix_max = lax.dynamic_slice(
            global_max, (my_beam, first_kv * group_size), (1, own_rows * group_size)
        )
        weight_suf = jnp.exp(score_suf - suffix_max.reshape(own_rows, group_size)[..., None])
        numerator = jnp.einsum(
            "rgs,rsd->rgd",
            weight_suf.astype(jnp.bfloat16),
            cache_values,
            preferred_element_type=jnp.float32,
        )
        numerator_suf = numerator.reshape(1, own_rows * group_size, head_dim)
        denominator_suf = jnp.sum(weight_suf, axis=2).reshape(1, own_rows * group_size)
        weigh_numerator = place_add(
            weigh_numerator, numerator_suf, (my_beam, first_kv * group_size, 0)
        )
        denominator = place_add(denominator, denominator_suf, (my_beam, first_kv * group_size))
        numerator, denominator = (weigh_numerator, denominator)
        numerator_own, denominator_own = (
            lax.psum_scatter(numerator, "head", scatter_dimension=1, tiled=True),
            lax.psum_scatter(denominator, "head", scatter_dimension=1, tiled=True),
        )
        attended = (
            (numerator_own / denominator_own[..., None])
            .reshape(beam_count, own_heads * head_dim)
            .astype(jnp.bfloat16)
        )
        summed = lax.psum_scatter(
            lax.dot_general(
                w_out, attended, (((0,), (1,)), ((), ())), preferred_element_type=jnp.float32
            ),
            "head",
            scatter_dimension=0,
            tiled=True,
        )
        results.append(summed.T.astype(jnp.bfloat16))
    return jnp.stack(results)


def solution(mesh):
    return jax.shard_map(
        local,
        mesh=mesh,
        in_specs=(
            P("groups", None, "head"),
            P(None, "head"),
            P(None, "head"),
            P("head", None),
            P(("groups", "head"), None),
            P(("groups", "head"), None),
            P(("groups", "head"), None, None),
            P(("groups", "head"), None, None),
            P("groups", None),
            P("groups"),
            P("groups", None),
        ),
        out_specs=P("groups", None, "head"),
        check_vma=False,
    )
```

profile of v0, /device:TPU:0, one launch (start us, length us, event | category | flops | bytes accessed | tf_op | source)
XLA Modules:
  0.0 715.6 jit_solution(8827558000696640487)
XLA Ops:
  12.4 23.8 %all-gather = bf16[1,16,8192]{2,1,0:T(8,128)(2,1)S(1)} all-gather(bf16[1,16,512]{2,1,0:T(8,128)(2,1)S(1)} %get-tuple-element.22), channel_id=2, replica_groups=mesh['groups'=2,'head'=16] {'head'}, dimensions={2}, use_global_device_ids=true | all-gather | bytes 278528 | tf_op jit(solution)/shard_map/all_gather | solution.py:86
  36.3 17.6 %all-gather.10.cloned.1.call-done = bf16[128,64,128]{2,0,1:T(8,128)(2,1)} async-done(((bf16[8,64,128]{2,0,1:T(8,128)(2,1)}), bf16[128,64,128]{2,0,1:T(8,128)(2,1)}) %all-gather.10.cloned.1.call-update) | async-done | bytes 2097168 | tf_op jit(solution)/shard_map/all_gather | solution.py:145
  56.6 4.6 convolution_convert_fusion.20
  61.2 20.4 %all_gather.46 = bf16[16,8192]{1,0:T(8,128)(2,1)S(1)} all-gather(bf16[16,512]{1,0:T(8,128)(2,1)S(1)} %convolution_convert_fusion.20), channel_id=1, replica_groups=mesh['groups'=2,'head'=16] {'head'}, dimensions={1}, use_global_device_ids=true | all-gather | bytes 278528 | tf_op jit(solution)/shard_map/all_gather | solution.py:93
  82.0 17.9 %all_gather.47 = bf16[16,2048]{1,0:T(8,128)(2,1)S(1)} all-gather(bf16[16,128]{1,0:T(8,128)(2,1)S(1)} %convolution_convert_fusion.25), channel_id=1, replica_groups=mesh['groups'=2,'head'=16] {'head'}, dimensions={1}, use_global_device_ids=true | all-gather | bytes 69632 | tf_op jit(solution)/shard_map/all_gather | solution.py:94
  100.5 19.9 %all-gather.1 = bf16[1,16,8192]{2,1,0:T(8,128)(2,1)S(1)} all-gather(bf16[1,16,512]{2,1,0:T(8,128)(2,1)S(1)} %get-tuple-element.24), channel_id=3, replica_groups=mesh['groups'=2,'head'=16] {'head'}, dimensions={2}, use_global_device_ids=true | all-gather | bytes 278528 | tf_op jit(solution)/shard_map/all_gather | solution.py:86
  120.8 17.7 %all_gather.52 = bf16[16,2048]{1,0:T(8,128)(2,1)S(1)} all-gather(bf16[16,128]{1,0:T(8,128)(2,1)S(1)} %convolution_convert_fusion.24), channel_id=1, replica_groups=mesh['groups'=2,'head'=16] {'head'}, dimensions={1}, use_global_device_ids=true | all-gather | bytes 69632 | tf_op jit(solution)/shard_map/all_gather | solution.py:94
  139.4 4.6 convolution_convert_fusion.17
  144.0 19.7 %all_gather.51 = bf16[16,8192]{1,0:T(8,128)(2,1)S(1)} all-gather(bf16[16,512]{1,0:T(8,128)(2,1)S(1)} %convolution_convert_fusion.17), channel_id=1, replica_groups=mesh['groups'=2,'head'=16] {'head'}, dimensions={1}, use_global_device_ids=true | all-gather | bytes 278528 | tf_op jit(solution)/shard_map/all_gather | solution.py:93
  175.6 18.1 %all-gather.2 = bf16[1,16,8192]{2,1,0:T(8,128)(2,1)S(1)} all-gather(bf16[1,16,512]{2,1,0:T(8,128)(2,1)S(1)} %get-tuple-element.23), channel_id=4, replica_groups=mesh['groups'=2,'head'=16] {'head'}, dimensions={2}, use_global_device_ids=true | all-gather | bytes 278528 | tf_op jit(solution)/shard_map/all_gather | solution.py:86
  193.7 4.6 convolution_convert_fusion.16
  198.3 19.9 %all_gather.56 = bf16[16,8192]{1,0:T(8,128)(2,1)S(1)} all-gather(bf16[16,512]{1,0:T(8,128)(2,1)S(1)} %convolution_convert_fusion.16), channel_id=1, replica_groups=mesh['groups'=2,'head'=16] {'head'}, dimensions={1}, use_global_device_ids=true | all-gather | bytes 278528 | tf_op jit(solution)/shard_map/all_gather | solution.py:93
  218.7 17.6 %all_gather.57 = bf16[16,2048]{1,0:T(8,128)(2,1)S(1)} all-gather(bf16[16,128]{1,0:T(8,128)(2,1)S(1)} %convolution_convert_fusion.23), channel_id=1, replica_groups=mesh['groups'=2,'head'=16] {'head'}, dimensions={1}, use_global_device_ids=true | all-gather | bytes 69632 | tf_op jit(solution)/shard_map/all_gather | solution.py:94
  258.7 23.2 %all-gather.18.cloned.1.call-done = bf16[128,64,128]{2,0,1:T(8,128)(2,1)} async-done(((bf16[8,64,128]{2,0,1:T(8,128)(2,1)}), bf16[128,64,128]{2,0,1:T(8,128)(2,1)}) %all-gather.18.cloned.1.call-update) | async-done | bytes 2097168 | tf_op jit(solution)/shard_map/all_gather | solution.py:145
  284.6 60.9 %all-reduce.4 = (f32[16,64]{0,1:T(8,128)S(1)}, f32[16,64]{0,1:T(8,128)S(1)}, f32[16,64]{0,1:T(8,128)S(1)}) all-reduce(f32[16,64]{0,1:T(8,128)S(1)} %dynamic_update_slice.76, f32[16,64]{0,1:T(8,128)S(1)} %dynamic_update_slice.70, f32[16,64]{0,1:T(8,128)S(1)} %dynamic_update_slice.64), channel_id=1, replica_groups=mesh['groups'=2,'head'=16] {'head'}, use_global_device_ids=true, to_apply=%region_28.29 | all-reduce | flops 3072 | bytes 24576 | tf_op jit(solution)/shard_map/pmax | solution.py:178
  372.2 58.7 %all-reduce.3 = (f32[16,64]{0,1:T(8,128)S(1)}, f32[16,64]{0,1:T(8,128)S(1)}, f32[16,64]{0,1:T(8,128)S(1)}) all-reduce(f32[16,64]{0,1:T(8,128)S(1)} %dynamic_update_slice.80, f32[16,64]{0,1:T(8,128)S(1)} %dynamic_update_slice.74, f32[16,64]{0,1:T(8,128)S(1)} %dynamic_update_slice.68), channel_id=12, replica_groups=mesh['groups'=2,'head'=16] {'head'}, use_global_device_ids=true, to_apply=%region_33.34.clone | all-reduce | flops 3072 | bytes 24576
  431.0 5.5 convolution_bitcast_fusion.2
  436.8 36.4 %reduce-scatter.11.cloned.1.call-done = f32[16,4,128]{2,0,1:T(8,128)} async-done(((f32[16,64,128]{2,0,1:T(8,128)}), f32[16,4,128]{2,0,1:T(8,128)}) %reduce-scatter.11.cloned.1.call-update) | async-done | bytes 32784 | tf_op jit(solution)/shard_map/reduce_scatter | solution.py:217
  473.2 5.5 convolution_bitcast_fusion.1
  478.7 52.8 %reduce-scatter.15.cloned.1.call-done = f32[16,4,128]{2,0,1:T(8,128)} async-done(((f32[16,64,128]{2,0,1:T(8,128)}), f32[16,4,128]{2,0,1:T(8,128)}) %reduce-scatter.15.cloned.1.call-update) | async-done | bytes 32784 | tf_op jit(solution)/shard_map/reduce_scatter | solution.py:217
  531.6 5.5 convolution_bitcast_fusion
  537.1 53.2 %reduce-scatter.9.cloned.1.call-done = f32[512,16]{0,1:T(8,128)} async-done(((f32[8192,16]{0,1:T(8,128)}), f32[512,16]{0,1:T(8,128)}) %reduce-scatter.9.cloned.1.call-update) | async-done | bytes 32784 | tf_op jit(solution)/shard_map/reduce_scatter | solution.py:225
  591.0 57.7 %reduce-scatter.13.cloned.1.call-done = f32[512,16]{0,1:T(8,128)} async-done(((f32[8192,16]{0,1:T(8,128)}), f32[512,16]{0,1:T(8,128)}) %reduce-scatter.13.cloned.1.call-update) | async-done | bytes 32784 | tf_op jit(solution)/shard_map/reduce_scatter | solution.py:225
  649.4 57.9 %reduce-scatter.17.cloned.1.call-done = f32[512,16]{0,1:T(8,128)} async-done(((f32[8192,16]{0,1:T(8,128)}), f32[512,16]{0,1:T(8,128)}) %reduce-scatter.17.cloned.1.call-update) | async-done | bytes 32784 | tf_op jit(solution)/shard_map/reduce_scatter | solution.py:225
  (221 shorter events, 77.1 us)
Async XLA Ops:
  6.5 75.1 %copy-start = (bf16[8192,128]{1,0:T(8,128)(2,1)S(1)}, bf16[8192,128]{1,0:T(8,128)(2,1)}, u32[]{:S(2)}) copy-start(bf16[8192,128]{1,0:T(8,128)(2,1)} %param.13) | copy-start | bytes 6291460
  6.5 47.3 %all-gather.10.cloned.1.call-start = ((), (), s32[]{:S(2)}) async-start(), calls=%async_computation.6 | async-start | bytes 2228224 | tf_op jit(solution)/shard_map/all_gather | solution.py:145
  8.4 157.6 %all-gather.12.cloned.1.call-start = ((), (), s32[]{:S(2)}) async-start(), calls=%async_computation.7 | async-start | bytes 2228224 | tf_op jit(solution)/shard_map/all_gather | solution.py:146
  10.1 229.4 %all-gather.14.cloned.1.call-start = ((), (), s32[]{:S(2)}) async-start(), calls=%async_computation.10 | async-start | bytes 2228224 | tf_op jit(solution)/shard_map/all_gather | solution.py:145
  11.0 25.3 %copy-start.19 = (s32[16]{0:T(128)}, s32[16]{0:T(128)S(1)}, u32[]{:S(2)}) copy-start(s32[16]{0:T(128)S(1)} %get-tuple-element.31) | copy-start | bytes 196
  11.0 127.6 %copy-start.18 = (s32[16]{0:T(128)}, s32[16]{0:T(128)S(1)}, u32[]{:S(2)}) copy-start(s32[16]{0:T(128)S(1)} %get-tuple-element.32) | copy-start | bytes 196
  11.0 127.8 %copy-start.13 = (s32[16]{0:T(128)}, s32[16]{0:T(128)S(1)}, u32[]{:S(2)}) copy-start(s32[16]{0:T(128)S(1)} %get-tuple-element.33) | copy-start | bytes 196
  56.5 199.3 %all-gather.16.cloned.1.call-start = ((), (), s32[]{:S(2)}) async-start(), calls=%async_computation.11 | async-start | bytes 2228224 | tf_op jit(solution)/shard_map/all_gather | solution.py:146
  81.6 18.5 %copy-start.4 = (bf16[768,1024]{1,0:T(8,128)(2,1)S(1)}, bf16[768,1024]{1,0:T(8,128)(2,1)}, u32[]{:S(2)}) copy-start(bf16[768,1024]{1,0:T(8,128)(2,1)} %param.15) | copy-start | bytes 4718596
  82.0 56.7 %copy-start.17 = (s32[16,4]{0,1:T(4,128)S(1)}, s32[16,4]{0,1:T(4,128)}, u32[]{:S(2)}) copy-start(s32[16,4]{0,1:T(4,128)} %param.19) | copy-start | bytes 772
  100.5 63.2 %copy-start.2 = (bf16[96,8,8,128]{3,2,1,0:T(8,128)(2,1)}, bf16[96,8,8,128]{3,2,1,0:T(8,128)(2,1)S(1)}, u32[]{:S(2)}) copy-start(bf16[96,8,8,128]{3,2,1,0:T(8,128)(2,1)S(1)} %copy.272) | copy-start | bytes 4718596
  138.6 98.3 %copy-start.11 = (s32[4]{0:T(128)}, s32[4]{0:T(128)S(1)}, u32[]{:S(2)}) copy-start(s32[4]{0:T(128)S(1)} %and_select_fusion) | copy-start | bytes 52
  168.7 113.3 %all-gather.18.cloned.1.call-start = ((), (), s32[]{:S(2)}) async-start(), calls=%async_computation.14 | async-start | bytes 2228224 | tf_op jit(solution)/shard_map/all_gather | solution.py:145
  198.3 38.9 %copy-start.3 = (bf16[96,8,8,128]{3,2,1,0:T(8,128)(2,1)S(1)}, bf16[96,8,8,128]{3,2,1,0:T(8,128)(2,1)}, u32[]{:S(2)}) copy-start(bf16[96,8,8,128]{3,2,1,0:T(8,128)(2,1)} %copy-done.2) | copy-start | bytes 4718596
  239.5 15.1 %copy-start.6 = (bf16[8,64,128]{2,0,1:T(8,128)(2,1)S(1)}, bf16[8,64,128]{2,0,1:T(8,128)(2,1)}, u32[]{:S(2)}) copy-start(bf16[8,64,128]{2,0,1:T(8,128)(2,1)} %convolution_convert_fusion.11) | copy-start | bytes 393220
  242.2 13.0 %copy-start.8 = (bf16[8,64,128]{2,0,1:T(8,128)(2,1)S(1)}, bf16[8,64,128]{2,0,1:T(8,128)(2,1)}, u32[]{:S(2)}) copy-start(bf16[8,64,128]{2,0,1:T(8,128)(2,1)} %convolution_convert_fusion.9) | copy-start | bytes 393220
  242.2 126.2 %all-gather.20.cloned.1.call-start = ((), (), s32[]{:S(2)}) async-start(), calls=%async_computation.15 | async-start | bytes 2228224 | tf_op jit(solution)/shard_map/all_gather | solution.py:146
  251.7 32.7 %copy-start.14 = (s32[8]{0:T(128)}, s32[8]{0:T(128)S(1)}, u32[]{:S(2)}) copy-start(s32[8]{0:T(128)S(1)} %multiply_add_fusion) | copy-start | bytes 100
  258.5 172.5 %reduce-scatter.7.cloned.1.call-start = ((), (), s32[]{:S(2)}) async-start(), calls=%async_computation.8 | async-start | bytes 557056 | tf_op jit(solution)/shard_map/reduce_scatter | solution.py:217
  361.1 112.1 %reduce-scatter.11.cloned.1.call-start = ((), (), s32[]{:S(2)}) async-start(), calls=%async_computation.12 | async-start | bytes 557056 | tf_op jit(solution)/shard_map/reduce_scatter | solution.py:217
  367.5 164.0 %reduce-scatter.15.cloned.1.call-start = ((), (), s32[]{:S(2)}) async-start(), calls=%async_computation.16 | async-start | bytes 557056 | tf_op jit(solution)/shard_map/reduce_scatter | solution.py:217
  371.9 218.3 %reduce-scatter.9.cloned.1.call-start = ((), (), s32[]{:S(2)}) async-start(), calls=%async_computation.9 | async-start | bytes 557056 | tf_op jit(solution)/shard_map/reduce_scatter | solution.py:225
  436.5 212.1 %reduce-scatter.13.cloned.1.call-start = ((), (), s32[]{:S(2)}) async-start(), calls=%async_computation.13 | async-start | bytes 557056 | tf_op jit(solution)/shard_map/reduce_scatter | solution.py:225
  478.7 228.7 %reduce-scatter.17.cloned.1.call-start = ((), (), s32[]{:S(2)}) async-start(), calls=%async_computation.17 | async-start | bytes 557056 | tf_op jit(solution)/shard_map/reduce_scatter | solution.py:225
  (8 other events, 26.3 us)
Sparse Core Ops, SparseCore 0:
  9.5 44.2 all-gather.9
  56.0 40.9 all-gather.11
  99.1 40.9 all-gather.13
  168.8 39.0 all-gather.15
  242.4 39.5 all-gather.17
  284.0 40.5 all-gather.19
  361.2 53.1 reduce-scatter.6
  418.3 54.8 reduce-scatter.10
  476.7 54.7 reduce-scatter.14
  535.4 54.7 reduce-scatter.8
  593.8 54.8 reduce-scatter.12
  652.5 54.8 reduce-scatter.16
where the time goes:
time: 717 us; the launch traced here: 716 us
  waiting for transfers between devices  299 us (42%)
  blocking collectives  295 us (41%)
  matrix products  74.4 us (10%)
  local copies, waits for them, and re-layouts  19.3 us (3%)
  between operations  14.8 us (2%)
  other arithmetic  12.5 us (2%)
    reduce_scatter x3, waiting for transfers between devices, local(): lax.psum_scatter(lax.dot_general(w_out, attended, (((0,), (1,)), ((), ())...  169 us
    reduce_scatter x3, waiting for transfers between devices, local(): lax.psum_scatter(numerator, 'head', scatter_dimension=1, tiled=True)  89.2 us
    all_gather x3, blocking collectives, local(): block_in = lax.all_gather(tokens, 'head', axis=1, tiled=True)  61.9 us
    pmax x1, blocking collectives, local(): global_max = lax.pmax(local_max, 'head')  60.9 us
    all_gather x3, blocking collectives, local(): lax.all_gather(query_local, 'head', axis=1, tiled=True)  60 us
    unnamed x1, blocking collectives  58.7 us
    all_gather x3, blocking collectives, local(): lax.all_gather(keyval_local, 'head', axis=1, tiled=True)  53.2 us
    all_gather x3, waiting for transfers between devices, local(): lax.all_gather(cache_keys, 'head', axis=0, tiled=True)  40.8 us
  transfers between devices with their start and end apart: 12, of which 7 were waited for; matrix products, arithmetic and copies ran while one was open for 14% of the time, Pallas kernels for 0%

commit v1 on v0

v1 whole, which is shorter than its diff:
```python
import functools
import math

import jax
import jax.numpy as jnp
from jax import lax
from jax.experimental import pallas as pl
from jax.experimental.pallas import tpu as pltpu
from jax.sharding import PartitionSpec as P

NEG = float("-inf")


def lookup(lookup_table, indices):
    row_count = lookup_table.shape[0]
    matches = indices[:, None] == jnp.arange(row_count, dtype=jnp.int32)[None, :]
    return jnp.sum(jnp.where(matches, lookup_table[None, :], 0), axis=1)


def reverse_bits(index, bits):
    total = 0
    for i in range(bits):
        total = total + ((index // (1 << i)) % 2) * (1 << (bits - 1 - i))
    return total


def masks(page_table, suffix_len, parents, my_beam, slots):
    steps, beams = parents.shape
    page_count = page_table.shape[1]
    page_size = slots // page_count
    beam_ids = jnp.arange(beams, dtype=jnp.int32)
    mine = beam_ids == my_beam
    own_pages = jnp.sum(jnp.where(mine[:, None], page_table, 0), axis=0)
    own_len = jnp.sum(jnp.where(mine, suffix_len, 0))
    page_ids = jnp.arange(page_count, dtype=jnp.int32)
    logical = jnp.sum(
        jnp.where(own_pages[:, None] == page_ids[None, :], page_ids[:, None], 0), axis=0
    )
    place = logical[:, None] * page_size + jnp.arange(page_size, dtype=jnp.int32)[None, :]
    slot_ok = place.reshape(slots) < own_len
    suffix_rows, fresh_rows = [], []
    for step in range(steps):
        current = beam_ids
        hits = [None] * steps
        hits[step] = current
        for later in range(step, 0, -1):
            current = lookup(parents[later], current)
            hits[later - 1] = current
        ancestor = lookup(parents[0], current)
        suffix_rows.append((ancestor == my_beam)[:, None] & slot_ok[None, :])
        fresh_rows.append(
            jnp.concatenate(
                [
                    jnp.zeros((beams, beams), bool)
                    if hit is None
                    else hit[:, None] == beam_ids[None, :]
                    for hit in hits
                ],
                axis=1,
            )
        )
    suffix_ok = jnp.concatenate(suffix_rows, axis=0)
    fresh_ok = jnp.concatenate(fresh_rows, axis=0)
    suffix_ok = jnp.pad(suffix_ok, ((0, 0), (0, 128 - suffix_ok.shape[1])))
    fresh_ok = jnp.pad(fresh_ok, ((0, 0), (0, 128 - fresh_ok.shape[1])))
    return jnp.where(jnp.stack([suffix_ok, fresh_ok]), 0.0, NEG).astype(jnp.float32)


def kernel(
    n,
    x_ref,
    sk_ref,
    sv_ref,
    mask_ref,
    wq_hbm,
    wkv_hbm,
    wo_hbm,
    pk_hbm,
    pv_hbm,
    out_ref,
    xg,
    qg,
    kvg,
    wq,
    wkv,
    wo,
    pk,
    pv,
    ske,
    sve,
    scores,
    fresh,
    maxes,
    max_in,
    acc,
    acc_in,
    y,
    y_in,
    proj_q,
    proj_kv,
    load_sem,
    send_sem,
    recv_sem,
):
    bits = n.bit_length() - 1
    me = lax.axis_index("head")
    pme = reverse_bits(me, bits)
    tokens, dl = x_ref.shape
    width_q = wq.shape[1]
    width_kv = wkv.shape[1]
    hd = 128
    hq = width_q // hd
    rows = hq * tokens
    own_rows, slots = sk_ref.shape[0], sk_ref.shape[1]
    kv_heads = pk.shape[1] // hd
    group_size = hq * n // kv_heads
    pre = pk.shape[0]
    scale = 1.0 / math.sqrt(hd)
    first_kv = me * own_rows % kv_heads
    blocks = -(-rows // 128)
    f32, bf16 = jnp.float32, jnp.bfloat16

    loads = [
        pltpu.make_async_copy(src, dst, load_sem.at[i])
        for i, (src, dst) in enumerate(
            ((wq_hbm, wq), (wkv_hbm, wkv), (pk_hbm, pk), (pv_hbm, pv), (wo_hbm, wo))
        )
    ]
    for load in loads:
        load.start()

    def bit(i):
        return (me // (1 << i)) % 2

    def partner(i):
        return me + (1 - 2 * bit(i)) * (1 << i)

    barrier = pltpu.get_barrier_semaphore()
    for i in range(bits):
        pl.semaphore_signal(
            barrier, inc=1, device_id={"head": partner(i)}, device_id_type=pl.DeviceIdType.MESH
        )

    xg[pme] = x_ref[...]
    for r in range(own_rows):
        zeros = jnp.zeros((hd - slots, hd), bf16)
        ske[r, :slots] = sk_ref[r]
        ske[r, slots:] = zeros
        sve[r, :slots] = sv_ref[r]
        sve[r, slots:] = zeros
    proj_q[...] = jnp.zeros_like(proj_q)
    proj_kv[...] = jnp.zeros_like(proj_kv)
    pl.semaphore_wait(barrier, bits)

    def send(src, dst, phase, step, i):
        copy = pltpu.make_async_remote_copy(
            src_ref=src,
            dst_ref=dst,
            send_sem=send_sem.at[phase, step],
            recv_sem=recv_sem.at[phase, step],
            device_id={"head": partner(i)},
            device_id_type=pl.DeviceIdType.MESH,
        )
        copy.start()
        return copy

    def gather_step(buf, phase, k):
        count = 1 << k
        base = (pme // count) * count
        part = buf.at[pl.ds(base, count)]
        return send(part, part, phase, k, bits - 1 - k)

    def gather_range(k):
        count = 1 << k
        base = (pme // count) * count
        return base + (1 - 2 * bit(bits - 1 - k)) * count, count

    def each(start, count, body):
        def run(i, carry):
            body(start + i)
            return carry

        lax.fori_loop(0, count, run, 0)

    def project(p):
        j = reverse_bits(p, bits)
        at = pl.ds(pl.multiple_of(j * dl, dl), dl)
        block = xg[p]
        proj_q[...] += jnp.dot(block, wq[at, :], preferred_element_type=f32)
        proj_kv[...] += jnp.dot(block, wkv[at, :], preferred_element_type=f32)

    start, count = pme, 1
    for k in range(bits):
        copy = gather_step(xg, 0, k)
        if k == 0:
            loads[0].wait()
            loads[1].wait()
        each(start, count, project)
        copy.wait()
        start, count = gather_range(k)
    each(start, count, project)

    for h in range(hq):
        qg[pme, h * tokens : (h + 1) * tokens, :] = proj_q[:, h * hd : (h + 1) * hd].astype(bf16)
    kvg[pme] = proj_kv[...].astype(bf16)

    row_id = lax.broadcasted_iota(jnp.int32, (rows, 128), 0)
    lane_id = lax.broadcasted_iota(jnp.int32, (rows, 128), 1)
    eye = row_id % 128 == lane_id

    def to_rows(column, fill, reduce):
        spread = jnp.where(eye, jnp.broadcast_to(column, (rows, 128)), fill)
        return [
            reduce(spread[i * 128 : min(rows, (i + 1) * 128)], axis=0, keepdims=True)
            for i in range(blocks)
        ]

    def to_column(parts, fill, reduce):
        return jnp.concatenate(
            [
                reduce(
                    jnp.where(
                        eye[: min(128, rows - i * 128)],
                        jnp.broadcast_to(part, (min(128, rows - i * 128), 128)),
                        fill,
                    ),
                    axis=1,
                    keepdims=True,
                )
                for i, part in enumerate(parts)
            ],
            axis=0,
        )

    def heads_of(p):
        kv = reverse_bits(p, bits) * hq // group_size
        off = kv - first_kv
        return kv, off

    suffix_mask = jnp.concatenate([mask_ref[0]] * hq, axis=0)

    def clip(off):
        return jnp.minimum(jnp.maximum(off, 0), own_rows - 1)

    def score(p):
        kv, off = heads_of(p)
        q = qg[p]
        keys = pk[:, pl.ds(pl.multiple_of(kv * hd, hd), hd)]
        nt = (((1,), (1,)), ((), ()))
        s = lax.dot_general(q, keys, nt, preferred_element_type=f32) * scale
        scores[p, :, :pre] = s
        hit = jnp.where((off >= 0) & (off < own_rows), 0.0, NEG)
        e = lax.dot_general(q, ske[clip(off)], nt, preferred_element_type=f32) * scale
        e = e + suffix_mask + hit
        scores[p, :, pre:] = e
        m = jnp.maximum(jnp.max(s, axis=1, keepdims=True), jnp.max(e, axis=1, keepdims=True))
        for i, part in enumerate(to_rows(m, NEG, jnp.max)):
            maxes[0, p, i : i + 1, :] = part

    start, count = pme, 1
    for k in range(bits):
        copies = (gather_step(qg, 1, k), gather_step(kvg, 2, k))
        if k == 0:
            loads[2].wait()
        each(start, count, score)
        for copy in copies:
            copy.wait()
        start, count = gather_range(k)
    each(start, count, score)

    own_kv = me * hq // group_size
    pieces = hd // width_kv if width_kv < hd else 1

    def fresh_block(column):
        if width_kv >= hd:
            j = column * hd // width_kv
            return kvg[reverse_bits(j, bits)]
        j = column * pieces
        return jnp.concatenate([kvg[reverse_bits(j + i, bits)] for i in range(pieces)], axis=1)

    fresh_keys = fresh_block(own_kv)
    fresh_values = fresh_block(own_kv + kv_heads)
    pad = jnp.zeros((hd - tokens, hd), bf16)
    fresh_keys = jnp.concatenate([fresh_keys, pad], axis=0)
    fresh_values = jnp.concatenate([fresh_values, pad], axis=0)
    f = lax.dot_general(
        qg[pme], fresh_keys, (((1,), (1,)), ((), ())), preferred_element_type=f32
    )
    f = f * scale + jnp.concatenate([mask_ref[1]] * hq, axis=0)
    fresh[...] = f
    for i, part in enumerate(to_rows(jnp.max(f, axis=1, keepdims=True), NEG, jnp.max)):
        maxes[0, pme, i : i + 1, :] = jnp.maximum(maxes[0, pme, i : i + 1, :], part)

    for k in range(bits):
        send(maxes.at[k], max_in.at[k], 3, k, k).wait()
        maxes[k + 1] = jnp.maximum(maxes[k], max_in[k])

    loads[3].wait()

    def largest(p):
        return to_column(
            [maxes[bits, p, i : i + 1, :] for i in range(blocks)], NEG, jnp.max
        )

    def put_totals(p, column):
        parts = to_rows(column, 0.0, jnp.sum)
        parts.append(jnp.zeros((8 - blocks, 128), f32))
        acc[p, rows:, :] = jnp.concatenate(parts, axis=0)

    def weigh(p):
        kv, off = heads_of(p)
        w = jnp.exp(scores[p] - largest(p))
        values = pv[:, pl.ds(pl.multiple_of(kv * hd, hd), hd)]
        wb = w.astype(bf16)
        acc[p, :rows, :] = jnp.dot(
            wb[:, :pre], values, preferred_element_type=f32
        ) + jnp.dot(wb[:, pre:], sve[clip(off)], preferred_element_type=f32)
        put_totals(p, jnp.sum(w, axis=1, keepdims=True))

    def scatter_sum(buf, buf_in, phase, fill, own_extra):
        offset = 0
        count = n // 2
        for k in range(bits):
            keep = (pme // count) * count
            away = keep + (1 - 2 * bit(k)) * count
            if k == 0:
                each(away, count, fill)
            else:
                before = offset - 2 * count
                prior = (pme // (2 * count)) * (2 * count)

                def add(p):
                    buf[p] += buf_in[before + p - prior]

                each(away, count, add)
            copy = send(
                buf.at[pl.ds(away, count)], buf_in.at[pl.ds(offset, count)], phase, k, k
            )
            if k == 0:
                each(keep, count, fill)
                own_extra()
            else:
                each(keep, count, add)
            copy.wait()
            offset += count
            count //= 2
        return buf[pme] + buf_in[offset - 1]

    def add_fresh():
        w = jnp.exp(fresh[...] - largest(pme))
        acc[pme, :rows, :] += jnp.dot(
            w.astype(bf16), fresh_values, preferred_element_type=f32
        )
        parts = to_rows(jnp.sum(w, axis=1, keepdims=True), 0.0, jnp.sum)
        parts.append(jnp.zeros((8 - blocks, 128), f32))
        acc[pme, rows:, :] += jnp.concatenate(parts, axis=0)

    total = scatter_sum(acc, acc_in, 4, weigh, add_fresh)
    column = to_column([total[rows + i : rows + i + 1] for i in range(blocks)], 0.0, jnp.sum)
    attended = (total[:rows] / column).astype(bf16)
    attended = jnp.concatenate(
        [attended[h * tokens : (h + 1) * tokens] for h in range(hq)], axis=1
    )
    loads[4].wait()

    def out_block(p):
        j = reverse_bits(p, bits)
        columns = wo[:, pl.ds(pl.multiple_of(j * dl, dl), dl)]
        y[p] = jnp.dot(attended, columns, preferred_element_type=f32)

    result = scatter_sum(y, y_in, 5, out_block, lambda: None)
    out_ref[...] = result.astype(bf16)


def local(
    inputs,
    w_query,
    w_keyval,
    w_out,
    prefix_keys,
    prefix_values,
    suffix_keys,
    suffix_values,
    page_table,
    suffix_len,
    parents,
):
    n = lax.axis_size("head")
    bits = n.bit_length() - 1
    me = lax.axis_index("head")
    steps, beams, dl = inputs.shape
    tokens = steps * beams
    own_rows, slots, hd = suffix_keys.shape
    kv_heads = prefix_keys.shape[1] // hd
    my_beam = me * own_rows // kv_heads
    width_q, width_kv = w_query.shape[1], w_keyval.shape[1]
    rows = width_q // hd * tokens
    blocks = -(-rows // 128)
    pre = prefix_keys.shape[0]
    mask = masks(page_table, suffix_len, parents, my_beam, slots)
    bf16, f32 = jnp.bfloat16, jnp.float32
    vmem = pl.BlockSpec(memory_space=pltpu.VMEM)
    hbm = pl.BlockSpec(memory_space=pl.ANY)
    out = pl.pallas_call(
        functools.partial(kernel, n),
        out_shape=jax.ShapeDtypeStruct((tokens, dl), bf16),
        in_specs=[vmem] * 4 + [hbm] * 5,
        out_specs=vmem,
        scratch_shapes=[
            pltpu.VMEM((n, tokens, dl), bf16),
            pltpu.VMEM((n, rows, hd), bf16),
            pltpu.VMEM((n, tokens, width_kv), bf16),
            pltpu.VMEM(w_query.shape, bf16),
            pltpu.VMEM(w_keyval.shape, bf16),
            pltpu.VMEM(w_out.shape, bf16),
            pltpu.VMEM(prefix_keys.shape, bf16),
            pltpu.VMEM(prefix_values.shape, bf16),
            pltpu.VMEM((own_rows, hd, hd), bf16),
            pltpu.VMEM((own_rows, hd, hd), bf16),
            pltpu.VMEM((n, rows, pre + hd), f32),
            pltpu.VMEM((rows, hd), f32),
            pltpu.VMEM((bits + 1, n, blocks, 128), f32),
            pltpu.VMEM((bits, n, blocks, 128), f32),
            pltpu.VMEM((n, rows + 8, hd), f32),
            pltpu.VMEM((n - 1, rows + 8, hd), f32),
            pltpu.VMEM((n, tokens, dl), f32),
            pltpu.VMEM((n - 1, tokens, dl), f32),
            pltpu.VMEM((tokens, width_q), f32),
            pltpu.VMEM((tokens, width_kv), f32),
            pltpu.SemaphoreType.DMA((5,)),
            pltpu.SemaphoreType.DMA((6, bits)),
            pltpu.SemaphoreType.DMA((6, bits)),
        ],
        compiler_params=pltpu.CompilerParams(
            collective_id=0, has_side_effects=True, vmem_limit_bytes=56 * 1024 * 1024
        ),
    )(
        inputs.reshape(tokens, dl),
        suffix_keys,
        suffix_values,
        mask,
        w_query,
        w_keyval,
        w_out,
        prefix_keys,
        prefix_values,
    )
    return out.reshape(steps, beams, dl)


def solution(mesh):
    return jax.shard_map(
        local,
        mesh=mesh,
        in_specs=(
            P("groups", None, "head"),
            P(None, "head"),
            P(None, "head"),
            P("head", None),
            P(("groups", "head"), None),
            P(("groups", "head"), None),
            P(("groups", "head"), None, None),
            P(("groups", "head"), None, None),
            P("groups", None),
            P("groups"),
            P("groups", None),
        ),
        out_specs=P("groups", None, "head"),
        check_vma=False,
    )
```

time: 717 us -> 112 us (0.16)
  waiting for transfers between devices: 299 us -> 0 us
  blocking collectives: 295 us -> 0 us
  Pallas kernels: 0 us -> 105 us
  matrix products: 74.4 us -> 0 us
  local copies, waits for them, and re-layouts: 19.3 us -> 2.33 us
  between operations: 14.8 us -> 0.05 us
  other arithmetic: 12.5 us -> 4.34 us
    reduce_scatter x6 -> x0, waiting for transfers between devices: 258 us -> none  [the longest x3 169 us: local(): lax.psum_scatter(lax.dot_general(w_out, attended, (((0,), (1,)), ((), ())...]
    all_gather x9 -> x0, blocking collectives: 175 us -> none  [the longest x3 61.9 us: local(): block_in = lax.all_gather(tokens, 'head', axis=1, tiled=True)]
    pallas_call x0 -> x1, Pallas kernels: none -> 105 us  [local(): pl.pallas_call(functools.partial(kernel, n), out_shape=jax.ShapeDtypeStru...]
    dot_general x46 -> x0, matrix products: 74.4 us -> none  [the longest x3 16.4 us: local(): lax.dot_general(w_out, attended, (((0,), (1,)), ((), ())), preferred_elem...]
    pmax x1 -> x0, blocking collectives: 60.9 us -> none  [local(): global_max = lax.pmax(local_max, 'head')]
    unnamed x1 -> x0, blocking collectives: 58.7 us -> none
    all_gather x6 -> x0, waiting for transfers between devices: 40.8 us -> none  [the longest x3 40.8 us: local(): lax.all_gather(cache_keys, 'head', axis=0, tiled=True)]
    unnamed x58 -> x1, local copies, waits for them, and re-layouts: 9.33 us -> 1.42 us
  transfers between devices with their start and end apart: 12 -> 0, of which waited for: 7 -> 0; matrix products, arithmetic and copies ran while one was open for 14% -> 0% of each run, Pallas kernels for 0% -> 0%
where the time goes in v1:
time: 112 us; the launch traced here: 111 us
  Pallas kernels  105 us (94%)
  other arithmetic  4.34 us (4%)
  local copies, waits for them, and re-layouts  2.33 us (2%)
    pallas_call x1, Pallas kernels, local(): pl.pallas_call(functools.partial(kernel, n), out_shape=jax.ShapeDtypeStru...  105 us

profile of v1, /device:TPU:0, one launch (start us, length us, event | category | flops | bytes accessed | tf_op | source)
XLA Modules:
  0.0 111.3 jit_solution(895036182915510443)
XLA Ops:
  0.0 1.3 %select_reduce_fusion.8 = s32[]{:T(128)} fusion(s32[16]{0:T(128)} %param.20, s32[]{:T(128)S(6)} %select_n.41), kind=kLoop, calls=%fused_computation.25 | loop fusion | flops 47 | bytes 72 | tf_op jit(solution)/shard_map/reduce_sum | solution.py:34
  1.3 0.8 slice_bitcast_fusion.2
  2.1 0.1 select_reduce_fusion.2
  2.2 0.2 select_reduce_fusion.4
  2.4 0.2 select_reduce_fusion.5
  2.6 0.8 select_reduce_fusion.7
  3.4 0.1 select_reduce_fusion.6
  3.5 0.7 add_compare_fusion
  4.2 0.1 lt.15
  4.3 0.1 iota_compare_fusion
  4.4 0.1 iota_compare_fusion.1
  4.5 0.1 fusion
  4.6 0.1 broadcast_and_fusion.2
  4.7 0.6 add_select_fusion.mask_ref
  5.3 104.6 %shard_map.109 = bf16[48,512]{1,0:T(8,128)(2,1)} custom-call(bf16[48,512]{1,0:T(8,128)(2,1)} %bitcast.13, bf16[8,64,128]{2,1,0:T(8,128)(2,1)} %sk_ref.1, bf16[8,64,128]{2,1,0:T(8,128)(2,1)} %sv_ref.1, f32[2,48,128]{2,1,0:T(8,128)} %add_select_fusion.mask_ref, bf16[8192,512]{1,0:T(8,128)(2,1)} %wq_hbm.1, bf16[8192,128]{1,0:T(8,128)(2,1)} %wkv_hbm.1, ...), custom_call_target="tpu_custom_call" | custom-call | tf_op jit(solution)/shard_map/pallas_call | solution.py:404
  109.9 1.4 %copy.13 = bf16[3,16,512]{2,1,0:T(8,128)(2,1)} copy(bf16[3,16,512]{2,1,0:T(8,128)(2,1)} %bitcast.12) | data formatting | bytes 98304
  (7 shorter events, 0.1 us)

commit v2 on v1

v2 whole, which is shorter than its diff:
```python
import functools
import math

import jax
import jax.numpy as jnp
from jax import lax
from jax.experimental import pallas as pl
from jax.experimental.pallas import tpu as pltpu
from jax.sharding import PartitionSpec as P

NEG = float("-inf")


def masks(table_ref, len_ref, parents_ref, my_beam, slots, steps):
    i32 = jnp.int32
    beams, page_count = table_ref.shape
    page_size = slots // page_count
    lane = lax.broadcasted_iota(i32, (beams, 128), 1)
    row = lax.broadcasted_iota(i32, (beams, 128), 0)
    own_pages = jnp.where(
        lax.broadcasted_iota(i32, (beams, page_count), 0) == my_beam, table_ref[...], 0
    )
    page_of = jnp.zeros((beams, 128), i32)
    for page in range(1, page_count):
        page_of = page_of + jnp.where(lane >= page * page_size, 1, 0)
    logical = jnp.zeros((beams, 128), i32)
    for page in range(1, page_count):
        physical = jnp.sum(own_pages[:, page : page + 1], axis=0, keepdims=True)
        logical = logical + jnp.where(page_of == physical, page, 0)
    beam_lane = lax.broadcasted_iota(i32, (1, beams), 1)
    own_len = jnp.sum(
        jnp.where(beam_lane == my_beam, len_ref[...], 0), axis=1, keepdims=True
    )
    place = logical * page_size + lane - page_of * page_size
    slot_ok = jnp.where((place < own_len) & (lane < slots), 1, 0)
    square_lane = lax.broadcasted_iota(i32, (beams, beams), 1)
    square_row = lax.broadcasted_iota(i32, (beams, beams), 0)

    def lookup(step, column):
        table = jnp.broadcast_to(parents_ref[step : step + 1, :], (beams, beams))
        return jnp.sum(jnp.where(square_lane == column, table, 0), axis=1, keepdims=True)

    first = jnp.sum(jnp.where(square_lane == square_row, square_lane, 0), axis=1, keepdims=True)
    suffix_rows, fresh_rows = [], []
    for step in range(steps):
        current = first
        fresh_ok = jnp.where(lane == current + step * beams, 1, 0)
        for later in range(step, 0, -1):
            current = lookup(later, current)
            fresh_ok = fresh_ok + jnp.where(lane == current + (later - 1) * beams, 1, 0)
        ancestor = lookup(0, current)
        suffix_rows.append(jnp.where(ancestor == my_beam, slot_ok, 0))
        fresh_rows.append(fresh_ok)
    to_mask = lambda parts: jnp.where(jnp.concatenate(parts, axis=0) > 0, 0.0, NEG)
    return to_mask(suffix_rows), to_mask(fresh_rows)


def kernel(
    n,
    x_ref,
    sk_ref,
    sv_ref,
    table_ref,
    len_ref,
    parents_ref,
    wq_hbm,
    wkv_hbm,
    wo_hbm,
    pk_hbm,
    pv_hbm,
    out_ref,
    xg,
    qg,
    kvg,
    wq,
    wkv,
    wo,
    pk,
    pv,
    ske,
    sve,
    scores,
    fresh,
    maxes,
    max_in,
    acc,
    acc_in,
    y,
    y_in,
    proj_q,
    proj_kv,
    mask_buf,
    load_sem,
    send_sem,
    recv_sem,
):
    outers = n // 4
    me = lax.axis_index("head")
    outer_id, mid_id, inner_id = me // 4, (me // 2) % 2, me % 2

    def block(d, e, f):
        high = 0
        for i in range(outers.bit_length() - 1):
            high = high + ((outer_id // (1 << i)) % 2 + (d // (1 << i)) % 2) % 2 * (1 << i)
        return high * 4 + (mid_id + e) % 2 * 2 + (inner_id + f) % 2

    tokens, dl = x_ref.shape
    width_q = wq.shape[1]
    width_kv = wkv.shape[1]
    hd = 128
    hq = width_q // hd
    rows = hq * tokens
    own_rows, slots = sk_ref.shape[0], sk_ref.shape[1]
    kv_heads = pk.shape[1] // hd
    group_size = hq * n // kv_heads
    pre = pk.shape[0]
    scale = 1.0 / math.sqrt(hd)
    first_kv = me * own_rows % kv_heads
    blocks = -(-rows // 128)
    f32, bf16 = jnp.float32, jnp.bfloat16

    loads = [
        pltpu.make_async_copy(src, dst, load_sem.at[i])
        for i, (src, dst) in enumerate(
            ((wq_hbm, wq), (wkv_hbm, wkv), (pk_hbm, pk), (pv_hbm, pv), (wo_hbm, wo))
        )
    ]
    for load in loads:
        load.start()

    barrier = pltpu.get_barrier_semaphore()

    def greet(device):
        pl.semaphore_signal(
            barrier, inc=1, device_id={"head": device}, device_id_type=pl.DeviceIdType.MESH
        )

    for e, f in ((0, 1), (1, 0), (1, 1)):
        greet(block(0, e, f))
    for d in range(1, outers):
        greet(block(d, 0, 0))

    xg[me] = x_ref[...]
    for r in range(own_rows):
        zeros = jnp.zeros((hd - slots, hd), bf16)
        ske[r, :slots] = sk_ref[r]
        ske[r, slots:] = zeros
        sve[r, :slots] = sv_ref[r]
        sve[r, slots:] = zeros
    proj_q[...] = jnp.zeros_like(proj_q)
    proj_kv[...] = jnp.zeros_like(proj_kv)
    pl.semaphore_wait(barrier, outers + 2)

    def message(src, dst, phase, slot, device):
        return pltpu.make_async_remote_copy(
            src_ref=src,
            dst_ref=dst,
            send_sem=send_sem.at[phase, slot],
            recv_sem=recv_sem.at[phase, slot],
            device_id={"head": device},
            device_id_type=pl.DeviceIdType.MESH,
        )

    def each(start, stop, body):
        def run(i, carry):
            body(i)
            return carry

        lax.fori_loop(start, stop, run, 0)

    def gather(bufs, phases, use):
        def to_outer(d):
            return [message(b.at[me], b.at[me], p, d, block(d, 0, 0)) for b, p in zip(bufs, phases)]

        def to_mid(d):
            j = block(d, 0, 0)
            return [
                message(b.at[j], b.at[j], p, outers + d, block(0, 1, 0))
                for b, p in zip(bufs, phases)
            ]

        def to_inner(d, e):
            j = block(d, e, 0)
            return [
                message(b.at[j], b.at[j], p, (2 + e) * outers + d, block(0, 0, 1))
                for b, p in zip(bufs, phases)
            ]

        def start(copies):
            for copy in copies:
                copy.start()

        def wait_recv(copies):
            for copy in copies:
                copy.wait_recv()

        def wait_send(copies):
            for copy in copies:
                copy.wait_send()

        each(1, outers, lambda d: start(to_outer(d)))
        start(to_mid(0))
        start(to_inner(0, 0))
        yield
        use(me)

        def from_outer(d):
            wait_recv(to_outer(d))
            start(to_mid(d))
            start(to_inner(d, 0))
            use(block(d, 0, 0))

        def from_mid(d):
            wait_recv(to_mid(d))
            start(to_inner(d, 1))
            use(block(d, 1, 0))

        def from_inner(i):
            wait_recv(to_inner(i % outers, i // outers))
            use(block(i % outers, i // outers, 1))

        each(1, outers, from_outer)
        each(0, outers, from_mid)
        each(0, 2 * outers, from_inner)
        each(1, outers, lambda d: wait_send(to_outer(d)))
        each(0, outers, lambda d: wait_send(to_mid(d)))
        each(0, 2 * outers, lambda i: wait_send(to_inner(i % outers, i // outers)))
        yield

    def project(p):
        at = pl.ds(pl.multiple_of(p * dl, dl), dl)
        tile = xg[p]
        proj_q[...] += jnp.dot(tile, wq[at, :], preferred_element_type=f32)
        proj_kv[...] += jnp.dot(tile, wkv[at, :], preferred_element_type=f32)

    steps = gather([xg], [0], project)
    next(steps)
    my_beam = me * own_rows // kv_heads
    suffix_mask, fresh_mask = masks(
        table_ref, len_ref, parents_ref, my_beam, slots, parents_ref.shape[0]
    )
    mask_buf[0] = suffix_mask
    mask_buf[1] = fresh_mask
    loads[0].wait()
    loads[1].wait()
    next(steps)

    for h in range(hq):
        qg[me, h * tokens : (h + 1) * tokens, :] = proj_q[:, h * hd : (h + 1) * hd].astype(bf16)
    kvg[me] = proj_kv[...].astype(bf16)

    row_id = lax.broadcasted_iota(jnp.int32, (rows, 128), 0)
    lane_id = lax.broadcasted_iota(jnp.int32, (rows, 128), 1)
    eye = row_id % 128 == lane_id

    def to_rows(column, fill, reduce):
        spread = jnp.where(eye, jnp.broadcast_to(column, (rows, 128)), fill)
        return [
            reduce(spread[i * 128 : min(rows, (i + 1) * 128)], axis=0, keepdims=True)
            for i in range(blocks)
        ]

    def to_column(parts, fill, reduce):
        return jnp.concatenate(
            [
                reduce(
                    jnp.where(
                        eye[: min(128, rows - i * 128)],
                        jnp.broadcast_to(part, (min(128, rows - i * 128), 128)),
                        fill,
                    ),
                    axis=1,
                    keepdims=True,
                )
                for i, part in enumerate(parts)
            ],
            axis=0,
        )

    def heads_of(p):
        kv = p * hq // group_size
        off = kv - first_kv
        return kv, off

    suffix_mask = jnp.concatenate([mask_buf[0]] * hq, axis=0)

    def clip(off):
        return jnp.minimum(jnp.maximum(off, 0), own_rows - 1)

    def score(p):
        kv, off = heads_of(p)
        q = qg[p]
        keys = pk[:, pl.ds(pl.multiple_of(kv * hd, hd), hd)]
        nt = (((1,), (1,)), ((), ()))
        s = lax.dot_general(q, keys, nt, preferred_element_type=f32) * scale
        scores[p, :, :pre] = s
        hit = jnp.where((off >= 0) & (off < own_rows), 0.0, NEG)
        e = lax.dot_general(q, ske[clip(off)], nt, preferred_element_type=f32) * scale
        e = e + suffix_mask + hit
        scores[p, :, pre:] = e
        m = jnp.maximum(jnp.max(s, axis=1, keepdims=True), jnp.max(e, axis=1, keepdims=True))
        for i, part in enumerate(to_rows(m, NEG, jnp.max)):
            maxes[0, p, i : i + 1, :] = part

    steps = gather([qg, kvg], [1, 2], score)
    next(steps)
    loads[2].wait()
    next(steps)

    own_kv = me * hq // group_size
    pieces = hd // width_kv if width_kv < hd else 1

    def fresh_block(column):
        if width_kv >= hd:
            j = column * hd // width_kv
            return kvg[j]
        j = column * pieces
        return jnp.concatenate([kvg[j + i] for i in range(pieces)], axis=1)

    fresh_keys = fresh_block(own_kv)
    fresh_values = fresh_block(own_kv + kv_heads)
    pad = jnp.zeros((hd - tokens, hd), bf16)
    fresh_keys = jnp.concatenate([fresh_keys, pad], axis=0)
    fresh_values = jnp.concatenate([fresh_values, pad], axis=0)
    f = lax.dot_general(
        qg[me], fresh_keys, (((1,), (1,)), ((), ())), preferred_element_type=f32
    )
    f = f * scale + jnp.concatenate([mask_buf[1]] * hq, axis=0)
    fresh[...] = f
    for i, part in enumerate(to_rows(jnp.max(f, axis=1, keepdims=True), NEG, jnp.max)):
        maxes[0, me, i : i + 1, :] = jnp.maximum(maxes[0, me, i : i + 1, :], part)

    near = [
        message(maxes.at[0], max_in.at[2 * e + f], 3, 2 * e + f, block(0, e, f))
        for e, f in ((0, 1), (1, 0), (1, 1))
    ]
    for copy in near:
        copy.start()
    for copy in near:
        copy.wait()
    maxes[1] = jnp.maximum(jnp.maximum(maxes[0], max_in[1]), jnp.maximum(max_in[2], max_in[3]))
    far = [
        message(maxes.at[1], max_in.at[4 + d], 3, 4 + d, block(d, 0, 0))
        for d in range(1, outers)
    ]
    for copy in far:
        copy.start()
    for copy in far:
        copy.wait()
    top = maxes[1]
    for d in range(1, outers):
        top = jnp.maximum(top, max_in[4 + d])
    maxes[2] = top

    loads[3].wait()

    def largest(p):
        return to_column(
            [maxes[2, p, i : i + 1, :] for i in range(blocks)], NEG, jnp.max
        )

    def put_totals(p, column):
        parts = to_rows(column, 0.0, jnp.sum)
        parts.append(jnp.zeros((8 - blocks, 128), f32))
        acc[p, rows:, :] = jnp.concatenate(parts, axis=0)

    def weigh(p):
        kv, off = heads_of(p)
        w = jnp.exp(scores[p] - largest(p))
        values = pv[:, pl.ds(pl.multiple_of(kv * hd, hd), hd)]
        wb = w.astype(bf16)
        acc[p, :rows, :] = jnp.dot(
            wb[:, :pre], values, preferred_element_type=f32
        ) + jnp.dot(wb[:, pre:], sve[clip(off)], preferred_element_type=f32)
        put_totals(p, jnp.sum(w, axis=1, keepdims=True))

    def scatter_sum(buf, buf_in, phase, fill, own_extra):
        def to_inner(d, e):
            slot = (2 + e) * outers + d
            return message(
                buf.at[block(d, e, 1)], buf_in.at[slot], phase, slot, block(0, 0, 1)
            )

        def to_mid(d):
            slot = outers + d
            return message(buf.at[block(d, 1, 0)], buf_in.at[slot], phase, slot, block(0, 1, 0))

        def to_outer(d):
            return message(buf.at[block(d, 0, 0)], buf_in.at[d], phase, d, block(d, 0, 0))

        def inner(i):
            d, e = outers - 1 - i % outers, 1 - i // outers
            fill(block(d, e, 1))
            to_inner(d, e).start()

        def mid(i):
            d = outers - 1 - i
            p = block(d, 1, 0)
            fill(p)
            to_inner(d, 1).wait_recv()
            buf[p] += buf_in[3 * outers + d]
            to_mid(d).start()

        def outer(i):
            d = outers - 1 - i
            p = block(d, 0, 0)
            to_inner(d, 0).wait_recv()
            to_mid(d).wait_recv()
            buf[p] += buf_in[2 * outers + d] + buf_in[outers + d]
            to_outer(d).start()

        each(0, 2 * outers, inner)
        each(0, outers, mid)
        each(0, outers, lambda i: fill(block(outers - 1 - i, 0, 0)))
        own_extra()
        each(0, outers - 1, outer)
        to_inner(0, 0).wait_recv()
        to_mid(0).wait_recv()
        total = buf[me] + buf_in[2 * outers] + buf_in[outers]
        for d in range(1, outers):
            to_outer(d).wait_recv()
            total = total + buf_in[d]
        each(0, 2 * outers, lambda i: to_inner(i % outers, i // outers).wait_send())
        each(0, outers, lambda d: to_mid(d).wait_send())
        each(1, outers, lambda d: to_outer(d).wait_send())
        return total

    def add_fresh():
        w = jnp.exp(fresh[...] - largest(me))
        acc[me, :rows, :] += jnp.dot(
            w.astype(bf16), fresh_values, preferred_element_type=f32
        )
        parts = to_rows(jnp.sum(w, axis=1, keepdims=True), 0.0, jnp.sum)
        parts.append(jnp.zeros((8 - blocks, 128), f32))
        acc[me, rows:, :] += jnp.concatenate(parts, axis=0)

    total = scatter_sum(acc, acc_in, 4, weigh, add_fresh)
    column = to_column([total[rows + i : rows + i + 1] for i in range(blocks)], 0.0, jnp.sum)
    attended = (total[:rows] / column).astype(bf16)
    attended = jnp.concatenate(
        [attended[h * tokens : (h + 1) * tokens] for h in range(hq)], axis=1
    )
    loads[4].wait()

    def out_block(p):
        columns = wo[:, pl.ds(pl.multiple_of(p * dl, dl), dl)]
        y[p] = jnp.dot(attended, columns, preferred_element_type=f32)

    result = scatter_sum(y, y_in, 5, out_block, lambda: None)
    out_ref[...] = result.astype(bf16)


def local(
    inputs,
    w_query,
    w_keyval,
    w_out,
    prefix_keys,
    prefix_values,
    suffix_keys,
    suffix_values,
    page_table,
    suffix_len,
    parents,
):
    n = lax.axis_size("head")
    steps, beams, dl = inputs.shape
    tokens = steps * beams
    own_rows, slots, hd = suffix_keys.shape
    width_q, width_kv = w_query.shape[1], w_keyval.shape[1]
    rows = width_q // hd * tokens
    blocks = -(-rows // 128)
    pre = prefix_keys.shape[0]
    bf16, f32 = jnp.bfloat16, jnp.float32
    vmem = pl.BlockSpec(memory_space=pltpu.VMEM)
    hbm = pl.BlockSpec(memory_space=pl.ANY)
    out = pl.pallas_call(
        functools.partial(kernel, n),
        out_shape=jax.ShapeDtypeStruct((tokens, dl), bf16),
        in_specs=[vmem] * 6 + [hbm] * 5,
        out_specs=vmem,
        scratch_shapes=[
            pltpu.VMEM((n, tokens, dl), bf16),
            pltpu.VMEM((n, rows, hd), bf16),
            pltpu.VMEM((n, tokens, width_kv), bf16),
            pltpu.VMEM(w_query.shape, bf16),
            pltpu.VMEM(w_keyval.shape, bf16),
            pltpu.VMEM(w_out.shape, bf16),
            pltpu.VMEM(prefix_keys.shape, bf16),
            pltpu.VMEM(prefix_values.shape, bf16),
            pltpu.VMEM((own_rows, hd, hd), bf16),
            pltpu.VMEM((own_rows, hd, hd), bf16),
            pltpu.VMEM((n, rows, pre + hd), f32),
            pltpu.VMEM((rows, hd), f32),
            pltpu.VMEM((3, n, blocks, 128), f32),
            pltpu.VMEM((4 + n // 4, n, blocks, 128), f32),
            pltpu.VMEM((n, rows + 8, hd), f32),
            pltpu.VMEM((n, rows + 8, hd), f32),
            pltpu.VMEM((n, tokens, dl), f32),
            pltpu.VMEM((n, tokens, dl), f32),
            pltpu.VMEM((tokens, width_q), f32),
            pltpu.VMEM((tokens, width_kv), f32),
            pltpu.VMEM((2, tokens, 128), f32),
            pltpu.SemaphoreType.DMA((5,)),
            pltpu.SemaphoreType.DMA((6, n)),
            pltpu.SemaphoreType.DMA((6, n)),
        ],
        compiler_params=pltpu.CompilerParams(
            collective_id=0, has_side_effects=True, vmem_limit_bytes=56 * 1024 * 1024
        ),
    )(
        inputs.reshape(tokens, dl),
        suffix_keys,
        suffix_values,
        page_table,
        suffix_len.reshape(1, -1),
        parents,
        w_query,
        w_keyval,
        w_out,
        prefix_keys,
        prefix_values,
    )
    return out.reshape(steps, beams, dl)


def solution(mesh):
    return jax.shard_map(
        local,
        mesh=mesh,
        in_specs=(
            P("groups", None, "head"),
            P(None, "head"),
            P(None, "head"),
            P("head", None),
            P(("groups", "head"), None),
            P(("groups", "head"), None),
            P(("groups", "head"), None, None),
            P(("groups", "head"), None, None),
            P("groups", None),
            P("groups"),
            P("groups", None),
        ),
        out_specs=P("groups", None, "head"),
        check_vma=False,
    )
```

time: 112 us -> 75.5 us (0.67)
  Pallas kernels: 105 us -> 72.5 us
  other arithmetic: 4.34 us -> 0 us
    pallas_call x1, Pallas kernels: 105 us -> 72.5 us  [local(): pl.pallas_call(functools.partial(kernel, n), out_shape=jax.ShapeDtypeStru...]
    reduce_sum x6 -> x0, other arithmetic: 2.66 us -> none  [the longest x1 1.29 us: masks(): own_len = jnp.sum(jnp.where(mine, suffix_len, 0))]
    unnamed x1 -> x2, local copies, waits for them, and re-layouts: 1.42 us -> 2.78 us
where the time goes in v2:
time: 75.5 us; the launch traced here: 75.3 us
  Pallas kernels  72.5 us (96%)
  local copies, waits for them, and re-layouts  2.78 us (4%)
    pallas_call x1, Pallas kernels, local(): pl.pallas_call(functools.partial(kernel, n), out_shape=jax.ShapeDtypeStru...  72.5 us
    unnamed x2, local copies, waits for them, and re-layouts  2.78 us

profile of v2, /device:TPU:0, one launch (start us, length us, event | category | flops | bytes accessed | tf_op | source)
XLA Modules:
  0.0 75.3 jit_solution(2806900996867910380)
XLA Ops:
  0.0 1.4 %copy.12.table_ref = s32[16,4]{1,0:T(8,128)} copy(s32[16,4]{0,1:T(4,128)} %param.19) | data formatting | bytes 512 | tf_op args[8]
  1.4 72.5 %shard_map.109 = bf16[48,512]{1,0:T(8,128)(2,1)} custom-call(bf16[48,512]{1,0:T(8,128)(2,1)} %bitcast.4, bf16[8,64,128]{2,1,0:T(8,128)(2,1)} %sk_ref.1, bf16[8,64,128]{2,1,0:T(8,128)(2,1)} %sv_ref.1, s32[16,4]{1,0:T(8,128)} %copy.12.table_ref, s32[1,16]{1,0:T(1,128)} %bitcast.5, s32[3,16]{1,0:T(4,128)} %parents_ref.1, bf16[8192,512]{1,0:T(8,128)(2,1)} %wq_hbm.1, ...), custom_call_target="tpu_custom_call" | custom-call | tf_op jit(solution)/shard_map/pallas_call | solution.py:477
  73.9 1.4 %copy.14 = bf16[3,16,512]{2,1,0:T(8,128)(2,1)} copy(bf16[3,16,512]{2,1,0:T(8,128)(2,1)} %bitcast.3) | data formatting | bytes 98304

commit v3 on v2

--- a/solution.py
+++ b/solution.py
@@ -13,21 +13,21 @@
 
 def masks(table_ref, len_ref, parents_ref, my_beam, slots, steps):
     i32 = jnp.int32
-    beams, page_count = table_ref.shape
+    page_count, beams = table_ref.shape
     page_size = slots // page_count
     lane = lax.broadcasted_iota(i32, (beams, 128), 1)
-    row = lax.broadcasted_iota(i32, (beams, 128), 0)
-    own_pages = jnp.where(
-        lax.broadcasted_iota(i32, (beams, page_count), 0) == my_beam, table_ref[...], 0
-    )
+    beam_lane = lax.broadcasted_iota(i32, (1, beams), 1)
     page_of = jnp.zeros((beams, 128), i32)
     for page in range(1, page_count):
         page_of = page_of + jnp.where(lane >= page * page_size, 1, 0)
     logical = jnp.zeros((beams, 128), i32)
     for page in range(1, page_count):
-        physical = jnp.sum(own_pages[:, page : page + 1], axis=0, keepdims=True)
+        physical = jnp.sum(
+            jnp.where(beam_lane == my_beam, table_ref[page : page + 1, :], 0),
+            axis=1,
+            keepdims=True,
+        )
         logical = logical + jnp.where(page_of == physical, page, 0)
-    beam_lane = lax.broadcasted_iota(i32, (1, beams), 1)
     own_len = jnp.sum(
         jnp.where(beam_lane == my_beam, len_ref[...], 0), axis=1, keepdims=True
     )
@@ -125,7 +125,7 @@
             ((wq_hbm, wq), (wkv_hbm, wkv), (pk_hbm, pk), (pv_hbm, pv), (wo_hbm, wo))
         )
     ]
-    for load in loads:
+    for load in loads[:2]:
         load.start()
 
     barrier = pltpu.get_barrier_semaphore()
@@ -243,6 +243,8 @@
     mask_buf[1] = fresh_mask
     loads[0].wait()
     loads[1].wait()
+    for load in loads[2:]:
+        load.start()
     next(steps)
 
     for h in range(hq):
@@ -330,12 +332,24 @@
     for i, part in enumerate(to_rows(jnp.max(f, axis=1, keepdims=True), NEG, jnp.max)):
         maxes[0, me, i : i + 1, :] = jnp.maximum(maxes[0, me, i : i + 1, :], part)
 
+    def put_totals(p, column):
+        parts = to_rows(column, 0.0, jnp.sum)
+        parts.append(jnp.zeros((8 - blocks, 128), f32))
+        acc[p, rows:, :] = jnp.concatenate(parts, axis=0)
+
+    def soften(p):
+        own = to_column([maxes[0, p, i : i + 1, :] for i in range(blocks)], NEG, jnp.max)
+        w = jnp.exp(scores[p] - own)
+        scores[p] = w
+        put_totals(p, jnp.sum(w, axis=1, keepdims=True))
+
     near = [
         message(maxes.at[0], max_in.at[2 * e + f], 3, 2 * e + f, block(0, e, f))
         for e, f in ((0, 1), (1, 0), (1, 1))
     ]
     for copy in near:
         copy.start()
+    each(0, n // 2, soften)
     for copy in near:
         copy.wait()
     maxes[1] = jnp.maximum(jnp.maximum(maxes[0], max_in[1]), jnp.maximum(max_in[2], max_in[3]))
@@ -345,12 +359,14 @@
     ]
     for copy in far:
         copy.start()
+    each(n // 2, n, soften)
     for copy in far:
         copy.wait()
     top = maxes[1]
     for d in range(1, outers):
         top = jnp.maximum(top, max_in[4 + d])
     maxes[2] = top
+    maxes[1] = jnp.exp(maxes[0] - top)
 
     loads[3].wait()
 
@@ -359,20 +375,19 @@
             [maxes[2, p, i : i + 1, :] for i in range(blocks)], NEG, jnp.max
         )
 
-    def put_totals(p, column):
-        parts = to_rows(column, 0.0, jnp.sum)
-        parts.append(jnp.zeros((8 - blocks, 128), f32))
-        acc[p, rows:, :] = jnp.concatenate(parts, axis=0)
-
     def weigh(p):
         kv, off = heads_of(p)
-        w = jnp.exp(scores[p] - largest(p))
+        factor = [maxes[1, p, i : i + 1, :] for i in range(blocks)]
+        w = scores[p] * to_column(factor, 0.0, jnp.sum)
         values = pv[:, pl.ds(pl.multiple_of(kv * hd, hd), hd)]
         wb = w.astype(bf16)
         acc[p, :rows, :] = jnp.dot(
             wb[:, :pre], values, preferred_element_type=f32
         ) + jnp.dot(wb[:, pre:], sve[clip(off)], preferred_element_type=f32)
-        put_totals(p, jnp.sum(w, axis=1, keepdims=True))
+        for i in range(blocks):
+            acc[p, rows + i : rows + i + 1, :] *= jnp.where(
+                lane_id[:1] < rows - i * 128, factor[i], 0.0
+            )
 
     def scatter_sum(buf, buf_in, phase, fill, own_extra):
         def to_inner(d, e):
@@ -388,18 +403,21 @@
         def to_outer(d):
             return message(buf.at[block(d, 0, 0)], buf_in.at[d], phase, d, block(d, 0, 0))
 
-        def inner(i):
-            d, e = outers - 1 - i % outers, 1 - i // outers
+        def inner(d, e):
             fill(block(d, e, 1))
             to_inner(d, e).start()
-
-        def mid(i):
-            d = outers - 1 - i
+            fill(block(d, e, 0))
+
+        def mid(d):
             p = block(d, 1, 0)
-            fill(p)
             to_inner(d, 1).wait_recv()
             buf[p] += buf_in[3 * outers + d]
             to_mid(d).start()
+
+        def first(i):
+            d = outers - 1 - i
+            inner(d, 1)
+            mid(d + 1)
 
         def outer(i):
             d = outers - 1 - i
@@ -409,9 +427,11 @@
             buf[p] += buf_in[2 * outers + d] + buf_in[outers + d]
             to_outer(d).start()
 
-        each(0, 2 * outers, inner)
-        each(0, outers, mid)
-        each(0, outers, lambda i: fill(block(outers - 1 - i, 0, 0)))
+        inner(outers - 1, 1)
+        each(1, outers, first)
+        inner(outers - 1, 0)
+        mid(0)
+        each(1, outers, lambda i: inner(outers - 1 - i, 0))
         own_extra()
         each(0, outers - 1, outer)
         to_inner(0, 0).wait_recv()
@@ -512,7 +532,7 @@
         inputs.reshape(tokens, dl),
         suffix_keys,
         suffix_values,
-        page_table,
+        page_table.T,
         suffix_len.reshape(1, -1),
         parents,
         w_query,

time: 75.5 us -> 74.2 us (0.983)
  local copies, waits for them, and re-layouts: 2.78 us -> 1.42 us
    unnamed x2 -> x1, local copies, waits for them, and re-layouts: 2.78 us -> 1.42 us
where the time goes in v3:
time: 74.2 us; the launch traced here: 74 us
  Pallas kernels  72.6 us (98%)
  local copies, waits for them, and re-layouts  1.42 us (2%)
    pallas_call x1, Pallas kernels, local(): pl.pallas_call(functools.partial(kernel, n), out_shape=jax.ShapeDtypeStru...  72.6 us

profile of v3, /device:TPU:0, one launch (start us, length us, event | category | flops | bytes accessed | tf_op | source)
XLA Modules:
  0.0 74.0 jit_solution(1253918742705944867)
XLA Ops:
  0.0 72.6 %shard_map.109 = bf16[48,512]{1,0:T(8,128)(2,1)} custom-call(bf16[48,512]{1,0:T(8,128)(2,1)} %bitcast.5, bf16[8,64,128]{2,1,0:T(8,128)(2,1)} %sk_ref.1, bf16[8,64,128]{2,1,0:T(8,128)(2,1)} %sv_ref.1, s32[4,16]{1,0:T(4,128)} %bitcast.6, s32[1,16]{1,0:T(1,128)} %bitcast.7, s32[3,16]{1,0:T(4,128)} %parents_ref.1, bf16[8192,512]{1,0:T(8,128)(2,1)} %wq_hbm.1, ...), custom_call_target="tpu_custom_call" | custom-call | tf_op jit(solution)/shard_map/pallas_call | solution.py:497
  72.6 1.4 %copy.13 = bf16[3,16,512]{2,1,0:T(8,128)(2,1)} copy(bf16[3,16,512]{2,1,0:T(8,128)(2,1)} %bitcast.4) | data formatting | bytes 98304
